TPU v7x, 128 devices: a whole 4x4x4 slice. The times are simulated.
128 devices in a mesh: sfc: 8 (over x, core), blk: 16 (over y, z).
Axes of the slice: x: 4, y: 4, z: 4, core: 2. Of those that a mesh axis runs over, the one named last changes fastest.
Arguments:
- xin: bfloat16 [2048, 16, 1024], P(('sfc', 'blk')), may hold values from -6 to 6
- send_slot: int32 [128, 128], P(('sfc', 'blk')), may hold values from 0 to 15
- near_blocks: bfloat16 [256, 1024, 1024], P(('sfc', 'blk')), may hold values from -0.1875 to 0.1875
- near_row: int32 [256], P(('sfc', 'blk')), may hold values from 0 to 255, as said below
- near_src: int32 [256], P(('sfc', 'blk')), may hold values from 0 to 127, as said below
- far_left: bfloat16 [19968, 32, 1024], P(('sfc', 'blk')), may hold values from -0.3125 to 0.3125
- far_right: bfloat16 [19968, 32, 1024], P(('sfc', 'blk')), may hold values from -0.1875 to 0.1875
- far_row: int32 [19968], P(('sfc', 'blk')), may hold values from 0 to 255, as said below
- far_src: int32 [19968], P(('sfc', 'blk')), may hold values from 0 to 127, as said below
Outputs:
- product: float32 [2048, 16, 1024], P(('sfc', 'blk'))
Inputs may be any that keep to these rules, and one draw needn't show every extreme that they name: On every device, its 2 near_src entries are the device itself and another device of its cluster group, and near_src and far_src together name every device at least once. `far_src`: see near_src. On every device, the output clusters of its blocks (near_row and far_row together) are exactly 8 of the 16 clusters of each device of its cluster group. `far_row`: see near_row.
All inputs are finite; a program needn't handle non-finite values.
Results may differ from a plain program's by a relative error of at most 0.0027.
Values may be sent and summed in bfloat16 or wider, within the bound.
A program may use at most 128 MiB of HBM per device.

v0:
```python
import jax
import jax.numpy as jnp
from jax import lax
from jax.sharding import PartitionSpec as P


def local(xin, send_slot, near_blocks, near_row, near_src, far_left, far_right, far_row, far_src):
    clusters = xin.shape[0]
    outgoing = xin[send_slot[0]]
    incoming = lax.all_to_all(outgoing, ("sfc", "blk"), split_axis=0, concat_axis=0, tiled=True)
    near_inputs = incoming[near_src]
    near_term = jnp.einsum(
        "bij,brj->bri", near_blocks, near_inputs, preferred_element_type=jnp.float32
    )
    far_inputs = incoming[far_src]
    projection = jnp.einsum(
        "bkj,brj->brk", far_right, far_inputs, preferred_element_type=jnp.float32
    ).astype(jnp.bfloat16)
    far_term = jnp.einsum("bki,brk->bri", far_left, projection, preferred_element_type=jnp.float32)
    members = lax.axis_size("blk")
    group_rows = clusters * members
    partial_value = jax.ops.segment_sum(near_term, near_row, num_segments=group_rows)
    partial_value = partial_value + jax.ops.segment_sum(far_term, far_row, num_segments=group_rows)
    return lax.psum_scatter(partial_value, "blk", scatter_dimension=0, tiled=True)


def solution(mesh):
    placed = (
        P(("sfc", "blk"), None, None),
        P(("sfc", "blk"), None),
        P(("sfc", "blk"), None, None),
        P(("sfc", "blk")),
        P(("sfc", "blk")),
        P(("sfc", "blk"), None, None),
        P(("sfc", "blk"), None, None),
        P(("sfc", "blk")),
        P(("sfc", "blk")),
    )
    return jax.shard_map(
        local, mesh=mesh, in_specs=placed, out_specs=P(("sfc", "blk"), None, None), check_vma=False
    )
```

profile of v0, /device:TPU:1, one launch (start us, length us, event | category | flops | bytes accessed | tf_op | source)
XLA Modules:
  0.0 272.4 jit_solution(17589953547936065744)
XLA Ops:
  6.5 0.0 copy-start
  6.5 0.0 copy-start.2
  6.5 0.0 copy-start.4
  6.5 0.7 fusion.1
  7.3 0.3 copy-done
  7.6 2.8 %gather_fusion = bf16[128,16,1024]{2,1,0:T(8,128)(2,1)} fusion(bf16[16,16,1024]{2,1,0:T(8,128)(2,1)S(1)} %copy-done, s32[1024]{0:T(1024)S(1)} %pad_clamp_fusion.2), kind=kCustom, calls=%fused_computation | custom fusion | bytes 8389120 | tf_op jit(solution)/shard_map/gather | solution.py:9
  10.4 12.0 %all-to-all-start = ((bf16[128,16,1024]{2,1,0:T(8,128)(2,1)}), bf16[128,16,1024]{2,1,0:T(8,128)(2,1)}, u32[]{:S(2)}, u32[]{:S(2)}) async-start(bf16[128,16,1024]{2,1,0:T(8,128)(2,1)} %gather_fusion), calls=%async_computation | async-start | bytes 8388608 | tf_op jit(solution)/shard_map/all_to_all | solution.py:10
  22.3 0.0 reduce-scatter.2.cloned.1.call-start
  22.4 0.0 copy-done.2
  22.4 0.0 copy-done.4
  22.4 0.1 pad_add_fusion
  22.5 0.0 copy-done.3
  22.5 0.0 copy-done.5
  22.5 51.8 %all-to-all-done = bf16[128,16,1024]{2,1,0:T(8,128)(2,1)} async-done(((bf16[128,16,1024]{2,1,0:T(8,128)(2,1)}), bf16[128,16,1024]{2,1,0:T(8,128)(2,1)}, u32[]{:S(2)}, u32[]{:S(2)}) %all-to-all-start) | async-done | bytes 4194336 | tf_op jit(solution)/shard_map/all_to_all | solution.py:10
  74.3 2.7 %gather_fusion.1 = bf16[2,16,1024]{2,1,0:T(8,128)(2,1)S(1)} fusion(bf16[128,16,1024]{2,1,0:T(8,128)(2,1)} %all-to-all-done, s32[1024]{0:T(1024)S(1)} %pad_clamp_fusion.1), kind=kCustom, calls=%fused_computation.1 | custom fusion | bytes 131080 | tf_op jit(solution)/shard_map/gather | solution.py:11
  77.1 3.4 %fusion.2 = f32[2,16,1024]{2,1,0:T(8,128)S(1)} fusion(bf16[2,16,1024]{2,1,0:T(8,128)(2,1)S(1)} %gather_fusion.1, bf16[2,1024,1024]{2,1,0:T(8,128)(2,1)} %param.11), kind=kOutput, calls=%fused_computation.15 | convolution fusion | flops 67108864 | bytes 4390912 | tf_op jit(solution)/shard_map/bij,brj->bri/dot_general | solution.py:12
  80.5 9.9 %gather_fusion.2 = bf16[156,16,1024]{2,1,0:T(8,128)(2,1)} fusion(bf16[128,16,1024]{2,1,0:T(8,128)(2,1)} %all-to-all-done, s32[1024]{0:T(1024)S(1)} %pad_clamp_fusion), kind=kCustom, calls=%fused_computation.2 | custom fusion | bytes 10224240 | tf_op jit(solution)/shard_map/gather | solution.py:15
  90.4 16.3 %fusion = f32[156,16,1024]{2,1,0:T(8,128)} fusion(bf16[156,32,1024]{2,1,0:T(8,128)(2,1)} %param.14, bf16[156,16,1024]{2,1,0:T(8,128)(2,1)} %gather_fusion.2, bf16[156,32,1024]{2,1,0:T(8,128)(2,1)} %param.15), kind=kOutput, calls=%fused_computation.6 | convolution fusion | flops 327235584 | bytes 35782656 | tf_op jit(solution)/shard_map/bki,brk->bri/dot_general | solution.py:19
  106.7 10.0 %pad_maximum_fusion = f32[158,16,1024]{2,1,0:T(8,128)} fusion(f32[156,16,1024]{2,1,0:T(8,128)} %fusion, f32[2,16,1024]{2,1,0:T(8,128)S(1)} %fusion.2), kind=kLoop, calls=%fused_computation.4 | loop fusion | flops 2588672 | bytes 20709376 | tf_op jit(solution)/shard_map/concatenate.1
  116.7 7.9 %broadcast.26 = f32[256,16,1024]{2,1,0:T(8,128)} broadcast(f32[]{:T(128)} %constant.4.clone.1), dimensions={} | broadcast | bytes 16777220 | tf_op jit(solution)/shard_map/broadcast.7
  124.5 33.2 %scatter_fusion = f32[256,16,1024]{2,1,0:T(8,128)} fusion(f32[256,16,1024]{2,1,0:T(8,128)} %broadcast.26, s32[158]{0:T(256)S(1)} %bitcast.12, f32[158,16,1024]{2,1,0:T(8,128)} %pad_maximum_fusion), kind=kCustom, calls=%fused_computation.3 | custom fusion | flops 2588672 | bytes 31064696 | tf_op jit(solution)/shard_map/add | solution.py:23
  157.7 0.0 reduce-scatter.2.cloned.1.call-update
  157.8 107.8 %reduce-scatter.2.cloned.1.call-done = f32[16,16,1024]{2,1,0:T(8,128)} async-done(((f32[256,16,1024]{2,1,0:T(8,128)}), f32[16,16,1024]{2,1,0:T(8,128)}) %reduce-scatter.2.cloned.1.call-update) | async-done | bytes 1048592 | tf_op jit(solution)/shard_map/reduce_scatter | solution.py:24
  265.6 0.0 copy-done.1
  (8 shorter events, 0.0 us)
Async XLA Ops:
  6.5 1.1 copy-start
  6.5 15.9 %copy-start.2 = (s32[156]{0:T(256)S(1)}, s32[156]{0:T(256)}, u32[]{:S(2)}) copy-start(s32[156]{0:T(256)} %param.16) | copy-start | bytes 1876
  6.5 15.9 %copy-start.4 = (s32[2]{0:T(128)S(1)}, s32[2]{0:T(128)}, u32[]{:S(2)}) copy-start(s32[2]{0:T(128)} %param.12) | copy-start | bytes 28
  6.5 16.0 %copy-start.3 = (s32[156]{0:T(256)S(1)}, s32[156]{0:T(256)}, u32[]{:S(2)}) copy-start(s32[156]{0:T(256)} %param.17) | copy-start | bytes 1876
  6.5 16.0 %copy-start.5 = (s32[2]{0:T(128)S(1)}, s32[2]{0:T(128)}, u32[]{:S(2)}) copy-start(s32[2]{0:T(128)} %param.13) | copy-start | bytes 28
  10.4 64.0 %all-to-all-start = ((bf16[128,16,1024]{2,1,0:T(8,128)(2,1)}), bf16[128,16,1024]{2,1,0:T(8,128)(2,1)}, u32[]{:S(2)}, u32[]{:S(2)}) async-start(bf16[128,16,1024]{2,1,0:T(8,128)(2,1)} %gather_fusion), calls=%async_computation | async-start | bytes 8388608 | tf_op jit(solution)/shard_map/all_to_all | solution.py:10
  22.3 243.2 %reduce-scatter.2.cloned.1.call-start = ((), (), s32[]{:S(2)}) async-start(), calls=%async_computation.2 | async-start | bytes 17825792 | tf_op jit(solution)/shard_map/reduce_scatter | solution.py:24
  124.5 141.1 %copy-start.1 = (bf16[16,16,1024]{2,1,0:T(8,128)(2,1)S(1)}, bf16[16,16,1024]{2,1,0:T(8,128)(2,1)}, u32[]{:S(2)}) copy-start(bf16[16,16,1024]{2,1,0:T(8,128)(2,1)} %param.9) | copy-start | bytes 1572868
Sparse Core Ops, SparseCore 0:
  157.9 107.6 reduce-scatter.1
where the time goes:
time: 273 us; the launch traced here: 272 us
  waiting for transfers between devices  160 us (59%)
  other arithmetic  44 us (16%)
  local copies, waits for them, and re-layouts  23.7 us (9%)
  matrix products  19.7 us (7%)
  between operations  13.5 us (5%)
  starting transfers between devices  12 us (4%)
    reduce_scatter x1, waiting for transfers between devices, local(): lax.psum_scatter(partial_value, 'blk', scatter_dimension=0, tiled=True)  108 us
    all_to_all x1, waiting for transfers between devices, local(): lax.all_to_all(outgoing, ('sfc', 'blk'), split_axis=0, concat_axis=0, til...  51.8 us
    add x1, other arithmetic, local(): partial_value + jax.ops.segment_sum(far_term, far_row, num_segments=group...  33.2 us
    dot_general x1, matrix products, local(): jnp.einsum('bki,brk->bri', far_left, projection, preferred_element_type=j...  16.3 us
    all_to_all x1, starting transfers between devices, local(): lax.all_to_all(outgoing, ('sfc', 'blk'), split_axis=0, concat_axis=0, til...  12 us
    another operation x1, other arithmetic  10 us
    gather x1, local copies, waits for them, and re-layouts, local(): far_inputs = incoming[far_src]  9.93 us
    another operation x1, local copies, waits for them, and re-layouts  7.86 us
  transfers between devices with their start and end apart: 2, of which 2 were waited for; matrix products, arithmetic and copies ran while one was open for 0% of the time, Pallas kernels for 0%

commit v1 on v0

v1 whole, which is shorter than its diff:
```python
import functools

import jax
import jax.numpy as jnp
from jax import lax
from jax.experimental import pallas as pl
from jax.experimental.pallas import tpu as pltpu
from jax.sharding import PartitionSpec as P

MESH = pl.DeviceIdType.MESH
BF = jnp.bfloat16
F32 = jnp.float32
I32 = jnp.int32
CL, RHS, LEAF, RANK = 16, 16, 1024, 32
NEAR, FAR, SLOTS = 2, 156, 8
ALL = NEAR + FAR
PAD = 160
HALF = LEAF // 2
COLS = ((0, 384), (384, 384), (768, 256))
ORDER = ((0, 1, 2), (1, 2, 0), (2, 0, 1))
FIRST = (1, 2)
SECOND = (2, 1)


def kernel(
    xin, slots_in, near_row, near_src, far_row, far_src, near_hbm, left_hbm, right_hbm,
    out,
    g0, g1, g2, slot_v, slot_s, t0, t1, t2, m0, m1, m2, inc,
    near, left, right, keys, tab_v, tab_s, inv_v, inv_r, inv_s,
    proj, term, cum, send0, send1, recv0, recv1, fold0, fold1, last0, last1,
    wsem, csem, s1s, s1r, sls, slr, s2s, s2r, s3s, s3r, ivs, ivr, o1s, o1r, o2s, o2r,
):
    sfc, blk = lax.axis_index("sfc"), lax.axis_index("blk")
    core = sfc % 2
    pos = (sfc // 2, blk // 4, blk % 4)

    def device(axis, where, flip=0):
        p = list(pos)
        p[axis] = where
        return (p[0] * 2 + (core + flip) % 2, p[1] * 4 + p[2])

    def ahead(axis, d):
        return (pos[axis] + d) % 4

    def remote(src, dst, ssem, rsem, to):
        return pltpu.make_async_remote_copy(
            src_ref=src, dst_ref=dst, send_sem=ssem, recv_sem=rsem, device_id=to, device_id_type=MESH
        )

    weights = [
        pltpu.make_async_copy(near_hbm, near, wsem.at[0]),
        pltpu.make_async_copy(right_hbm, right.at[pl.ds(0, FAR)], wsem.at[1]),
        pltpu.make_async_copy(left_hbm, left.at[pl.ds(0, FAR)], wsem.at[2]),
    ]

    barrier = pltpu.get_barrier_semaphore()
    peers = [device(0, pos[0], 1)]
    for axis in range(3):
        for d in range(1, 4):
            for flip in range(2):
                peers.append(device(axis, ahead(axis, d), flip))
    for to in peers:
        pl.semaphore_signal(barrier, inc=1, device_id=to, device_id_type=MESH)
    pl.semaphore_wait(barrier, len(peers))

    got = (g0, g1, g2)
    stage1, local1 = [], []
    for k in range(3):
        first = ORDER[k][0]
        lo, wide = COLS[k]
        part = xin.at[:, :, pl.ds(lo, wide)]
        mine = got[k].at[pos[first]]
        sends = []
        for d in range(1, 4):
            to = device(first, ahead(first, d))
            a = remote(slots_in, slot_v.at[k, pos[first]], sls.at[k, d - 1], slr.at[k, d - 1], to)
            b = remote(part, mine, s1s.at[k, d - 1], s1r.at[k, d - 1], to)
            a.start()
            b.start()
            sends += [a, b]
        own = [
            pltpu.make_async_copy(slots_in, slot_v.at[k, pos[first]], csem.at[2 * k]),
            pltpu.make_async_copy(part, mine, csem.at[2 * k + 1]),
        ]
        for c in own:
            c.start()
        stage1.append(sends)
        local1.append(own)
    for c in weights:
        c.start()

    right[FAR:PAD] = jnp.zeros((PAD - FAR, RANK, LEAF), BF)
    left[FAR:PAD] = jnp.zeros((PAD - FAR, RANK, LEAF), BF)

    def fill_far(j, _):
        keys[pl.ds(j, 1), :] = jnp.full((1, 256), far_row[j], I32)
        return 0

    lax.fori_loop(0, FAR, fill_far, 0)
    for j in range(NEAR):
        keys[FAR + j : FAR + j + 1, :] = jnp.full((1, 256), near_row[j], I32)
    keys[ALL:PAD, :] = jnp.full((PAD - ALL, 256), 300, I32)
    row_c = keys[...]
    down = lax.broadcasted_iota(I32, (PAD, 256), 0)
    lane = lax.broadcasted_iota(I32, (PAD, 256), 1)
    row_r = jnp.sum(jnp.where(down == lane, row_c, 0), axis=0, keepdims=True)
    real = lane < PAD
    same = real & (row_r == row_c)
    less = real & (row_r < row_c)
    first_r = jnp.sum(jnp.where(same & (down < lane), 1, 0), axis=0, keepdims=True) == 0
    place = jnp.sum(jnp.where(less | (same & (lane < down)), 1, 0), axis=1, keepdims=True)
    final = jnp.sum(jnp.where(less | same, 1, 0), axis=1, keepdims=True) - 1
    slot = jnp.sum(jnp.where(less & first_r, 1, 0), axis=1, keepdims=True)
    here = place == lane
    order = jnp.sum(jnp.where(here, down, 0), axis=0, keepdims=True)
    sorted_row = jnp.sum(jnp.where(here, row_c, 0), axis=0, keepdims=True)
    ends = jnp.max(jnp.where(slot == lane, final, 0), axis=0, keepdims=True)
    seat = jnp.max(jnp.where(row_c == lane, 8 - (slot & 7), 0), axis=0, keepdims=True)
    tab_v[0:1, :] = order
    tab_v[1:2, :] = sorted_row
    tab_v[2:3, :] = ends
    inv_v[0:1, :] = 8 - seat
    tab_copy = pltpu.make_async_copy(tab_v, tab_s, csem.at[6])
    tab_copy.start()
    places = []
    for h in range(2):
        axis = FIRST[h]
        for d in range(1, 4):
            c = remote(inv_v, inv_r.at[h, pos[axis]], ivs.at[h, d - 1], ivr.at[h, d - 1], device(axis, ahead(axis, d)))
            c.start()
            places.append(c)
        c = pltpu.make_async_copy(inv_v, inv_r.at[h, pos[axis]], csem.at[7 + h])
        c.start()
        places.append(c)
    recv = (recv0, recv1)
    for h in range(2):
        recv[h][:, :, SLOTS] = jnp.zeros((4, 4, RHS, HALF), BF)

    pick, mid = (t0, t1, t2), (m0, m1, m2)
    stage2 = []
    for k in (2, 0, 1):
        _, second, third = ORDER[k]
        for c in stage1[k]:
            c.wait_recv()
        for c in local1[k]:
            c.wait()
        copy = pltpu.make_async_copy(slot_v.at[k], slot_s.at[k], csem.at[9 + k])
        copy.start()
        copy.wait()

        def chosen(i, there, k=k, second=second, third=third):
            a, c, co = i // 8, (i // 2) % 4, i % 2
            p = list(pos)
            p[second] = there
            p[third] = c
            where = (p[0] * 2 + co) * 16 + p[1] * 4 + p[2]
            return a, c, co, got[k][a, slot_s[k, a, 0, where]]

        for d in range(1, 4):
            there = ahead(second, d)

            def put(i, _, k=k, d=d, there=there, chosen=chosen):
                a, c, co, value = chosen(i, there)
                pick[k][d - 1, a, c, co] = value
                return 0

            lax.fori_loop(0, 32, put, 0, unroll=4)
            dst = mid[k].at[pos[second]] if k == 2 else mid[k].at[:, pos[second]]
            c = remote(pick[k].at[d - 1], dst, s2s.at[k, d - 1], s2r.at[k, d - 1], device(second, there))
            c.start()
            stage2.append((k, c))

        def keep(i, _, k=k, second=second, chosen=chosen):
            a, c, co, value = chosen(i, pos[second])
            if k == 2:
                mid[k][pos[second], a, c, co] = value
            else:
                mid[k][a, pos[second], c, co] = value
            return 0

        lax.fori_loop(0, 32, keep, 0, unroll=4)

    stage3, local3 = [], []
    for k in (2, 0, 1):
        third = ORDER[k][2]
        lo, wide = COLS[k]
        for kk, c in stage2:
            if kk == k:
                c.wait_recv()
        cols = pl.ds(lo, wide)
        if k == 0:
            dst = inc.at[:, core, :, pos[2], :, cols]
        elif k == 1:
            dst = inc.at[pos[0], core, :, :, :, cols]
        else:
            dst = inc.at[:, core, pos[1], :, :, cols]
        for d in (1, 3, 2, 0):
            there = ahead(third, d)
            for flip in range(2):
                src = mid[k].at[:, :, there, (core + flip) % 2]
                if d == 0 and flip == 0:
                    c = pltpu.make_async_copy(src, dst, csem.at[12 + k])
                    local3.append(c)
                else:
                    n = d * 2 + flip - 1
                    c = remote(src, dst, s3s.at[k, n], s3r.at[k, n], device(third, there, flip))
                    stage3.append(c)
                c.start()
    tab_copy.wait()
    for c in weights:
        c.wait()
    for c in stage3:
        c.wait_recv()
    for c in local3:
        c.wait()

    def cluster(s):
        return inc[s >> 5, (s >> 4) & 1, (s >> 2) & 3, s & 3]

    diag = lax.broadcasted_iota(I32, (128, 256), 0) // 16 == lax.broadcasted_iota(I32, (128, 256), 1) // 32

    def project(g, _):
        x = jnp.concatenate([cluster(far_src[jnp.minimum(8 * g + e, FAR - 1)]) for e in range(8)], axis=0)
        w = right[pl.ds(8 * g, 8)].reshape(256, LEAF)
        r = lax.dot_general(x, w, (((1,), (1,)), ((), ())), preferred_element_type=F32)
        proj[g] = jnp.where(diag, r, 0.0).astype(BF)
        return 0

    lax.fori_loop(0, PAD // 8, project, 0)

    send = (send0, send1)
    out1 = []
    for h in range(2):
        first, second = FIRST[h], SECOND[h]
        cols = pl.ds(HALF * h, HALF)

        def far(g, _, cols=cols):
            w = left[pl.ds(8 * g, 8), :, cols].reshape(256, HALF)
            t = jnp.dot(proj[g], w, preferred_element_type=F32)
            term[pl.ds(8 * g, 8)] = t.reshape(8, RHS, HALF)
            return 0

        lax.fori_loop(0, PAD // 8, far, 0)
        for n in range(NEAR):
            w = near[n, HALF * h : HALF * (h + 1), :]
            term[FAR + n] = lax.dot_general(
                cluster(near_src[n]), w, (((1,), (1,)), ((), ())), preferred_element_type=F32
            )

        def scan(q, carry):
            value, before = carry
            row = tab_s[1, q]
            keep = (row == before).astype(F32)
            value = value * keep + term[tab_s[0, q]]
            cum[q] = value.astype(BF)
            return value, row

        lax.fori_loop(0, ALL, scan, (jnp.zeros((RHS, HALF), F32), jnp.int32(-1)), unroll=2)

        for d in (1, 3, 2, 0):
            there = ahead(first, d)

            def load(i, _, h=h, there=there):
                w, t = i // 8, i % 8
                p = there * 4 + w if h == 0 else w * 4 + there
                value = cum[tab_s[2, p * 8 + t]]
                if d == 0:
                    recv[h][there, w, t] = value
                else:
                    send[h][d - 1, w, t] = value
                return 0

            lax.fori_loop(0, 32, load, 0, unroll=4)
            if d:
                c = remote(
                    send[h].at[d - 1], recv[h].at[pos[first], :, pl.ds(0, SLOTS)],
                    o1s.at[h, d - 1], o1r.at[h, d - 1], device(first, there),
                )
                c.start()
                out1.append((h, c))

    for c in places:
        c.wait()
    inv_copy = pltpu.make_async_copy(inv_r, inv_s, csem.at[15])
    inv_copy.start()
    inv_copy.wait()

    fold, last = (fold0, fold1), (last0, last1)
    out2 = []
    for h in range(2):
        first, second = FIRST[h], SECOND[h]
        for hh, c in out1:
            if hh == h:
                c.wait_recv()
        for d in (1, 3, 2, 0):
            there = ahead(second, d)
            p = pos[first] * 4 + there if h == 0 else there * 4 + pos[first]

            def add(r, _, h=h, there=there, p=p, d=d):
                total = recv[h][0, there, inv_s[h, 0, 0, p * 16 + r]].astype(F32)
                for s in range(1, 4):
                    total += recv[h][s, there, inv_s[h, s, 0, p * 16 + r]].astype(F32)
                if d == 0:
                    out[r, :, HALF * h : HALF * (h + 1)] = total
                else:
                    fold[h][d - 1, r] = total.astype(BF)
                return 0

            lax.fori_loop(0, CL, add, 0, unroll=2)
            if d:
                c = remote(
                    fold[h].at[d - 1], last[h].at[d - 1],
                    o2s.at[h, d - 1], o2r.at[h, d - 1], device(second, there),
                )
                c.start()
                out2.append((h, c))
    for h in range(2):
        for hh, c in out2:
            if hh == h:
                c.wait_recv()

        def finish(r, _, h=h):
            cols = slice(HALF * h, HALF * (h + 1))
            total = out[r, :, cols]
            for s in range(3):
                total += last[h][s, r].astype(F32)
            out[r, :, cols] = total
            return 0

        lax.fori_loop(0, CL, finish, 0, unroll=2)

    for c in sum(stage1, []) + [c for _, c in stage2 + out1 + out2] + stage3:
        c.wait_send()


def local(xin, send_slot, near_blocks, near_row, near_src, far_left, far_right, far_row, far_src):
    vmem, smem = pl.BlockSpec(memory_space=pltpu.VMEM), pl.BlockSpec(memory_space=pltpu.SMEM)
    hbm = pl.BlockSpec(memory_space=pl.ANY)
    widths = [w for _, w in COLS]
    dma = pltpu.SemaphoreType.DMA
    scratch = [pltpu.VMEM((4, CL, RHS, w), BF) for w in widths]
    scratch += [pltpu.VMEM((3, 4, 1, 128), I32), pltpu.SMEM((3, 4, 1, 128), I32)]
    scratch += [pltpu.VMEM((3, 4, 4, 2, RHS, w), BF) for w in widths]
    scratch += [pltpu.VMEM((4, 4, 4, 2, RHS, w), BF) for w in widths]
    scratch += [pltpu.VMEM((4, 2, 4, 4, RHS, LEAF), BF)]
    scratch += [
        pltpu.VMEM((NEAR, LEAF, LEAF), BF),
        pltpu.VMEM((PAD, RANK, LEAF), BF),
        pltpu.VMEM((PAD, RANK, LEAF), BF),
        pltpu.VMEM((PAD, 256), I32),
        pltpu.VMEM((8, 256), I32),
        pltpu.SMEM((8, 256), I32),
        pltpu.VMEM((1, 256), I32),
        pltpu.VMEM((2, 4, 1, 256), I32),
        pltpu.SMEM((2, 4, 1, 256), I32),
        pltpu.VMEM((PAD // 8, 128, 256), BF),
        pltpu.VMEM((PAD, RHS, HALF), F32),
        pltpu.VMEM((PAD, RHS, HALF), BF),
    ]
    scratch += [pltpu.VMEM((3, 4, SLOTS, RHS, HALF), BF)] * 2
    scratch += [pltpu.VMEM((4, 4, SLOTS + 1, RHS, HALF), BF)] * 2
    scratch += [pltpu.VMEM((3, CL, RHS, HALF), BF)] * 4
    scratch += [dma((3,)), dma((16,)), dma((3, 3)), dma((3, 3)), dma((3, 3)), dma((3, 3)), dma((3, 3)), dma((3, 3))]
    scratch += [dma((3, 7)), dma((3, 7))] + [dma((2, 3))] * 6
    return pl.pallas_call(
        kernel,
        out_shape=jax.ShapeDtypeStruct((CL, RHS, LEAF), F32),
        in_specs=[vmem, vmem, smem, smem, smem, smem, hbm, hbm, hbm],
        out_specs=vmem,
        scratch_shapes=scratch,
        compiler_params=pltpu.CompilerParams(
            collective_id=0, has_side_effects=True, vmem_limit_bytes=62 << 20
        ),
        cost_estimate=pl.CostEstimate(flops=800_000_000, bytes_accessed=26_000_000, transcendentals=0),
        name="hmatrix",
    )(xin, send_slot, near_row, near_src, far_row, far_src, near_blocks, far_left, far_right)


def solution(mesh):
    both = ("sfc", "blk")
    placed = (
        P(both, None, None), P(both, None), P(both, None, None), P(both), P(both),
        P(both, None, None), P(both, None, None), P(both), P(both),
    )
    return jax.shard_map(local, mesh=mesh, in_specs=placed, out_specs=P(both, None, None), check_vma=False)
```

time: 273 us -> 126 us (0.46)
  waiting for transfers between devices: 160 us -> 0 us
  Pallas kernels: 0 us -> 123 us
  other arithmetic: 44 us -> 0 us
  local copies, waits for them, and re-layouts: 23.7 us -> 2.31 us
  matrix products: 19.7 us -> 0 us
  between operations: 13.5 us -> 0.01 us
  starting transfers between devices: 12 us -> 0 us
    pallas_call x0 -> x1, Pallas kernels: none -> 123 us  [local(): pl.pallas_call(kernel, out_shape=jax.ShapeDtypeStruct((CL, RHS, LEAF), F3...]
    reduce_scatter x1 -> x0, waiting for transfers between devices: 108 us -> none  [local(): lax.psum_scatter(partial_value, 'blk', scatter_dimension=0, tiled=True)]
    all_to_all x1 -> x0, waiting for transfers between devices: 51.8 us -> none  [local(): lax.all_to_all(outgoing, ('sfc', 'blk'), split_axis=0, concat_axis=0, til...]
    add x1 -> x0, other arithmetic: 33.2 us -> none  [local(): partial_value + jax.ops.segment_sum(far_term, far_row, num_segments=group...]
    dot_general x2 -> x0, matrix products: 19.7 us -> none  [the longest x1 16.3 us: local(): jnp.einsum('bki,brk->bri', far_left, projection, preferred_element_type=j...]
    gather x3 -> x0, local copies, waits for them, and re-layouts: 15.5 us -> none  [the longest x1 9.93 us: local(): far_inputs = incoming[far_src]]
    all_to_all x1 -> x0, starting transfers between devices: 12 us -> none  [local(): lax.all_to_all(outgoing, ('sfc', 'blk'), split_axis=0, concat_axis=0, til...]
    another operation x1 -> x0, other arithmetic: 10 us -> none
  transfers between devices with their start and end apart: 2 -> 0, of which waited for: 2 -> 0; matrix products, arithmetic and copies ran while one was open for 0% -> 0% of each run, Pallas kernels for 0% -> 0%
where the time goes in v1:
time: 126 us; the launch traced here: 125 us
  Pallas kernels  123 us (98%)
  local copies, waits for them, and re-layouts  2.31 us (2%)
    pallas_call x1, Pallas kernels, local(): pl.pallas_call(kernel, out_shape=jax.ShapeDtypeStruct((CL, RHS, LEAF), F3...  123 us

profile of v1, /device:TPU:1, one launch (start us, length us, event | category | flops | bytes accessed | tf_op | source)
XLA Modules:
  0.0 125.5 jit_solution(13183744735489611783)
XLA Ops:
  0.0 123.2 %hmatrix.1 = f32[16,16,1024]{2,1,0:T(8,128)} custom-call(bf16[16,16,1024]{2,1,0:T(8,128)(2,1)} %xin.1, s32[1,128]{1,0:T(1,128)} %slots_in.1, s32[2]{0:T(128)} %near_row.1, s32[2]{0:T(128)} %near_src.1, s32[156]{0:T(256)} %far_row.1, s32[156]{0:T(256)} %far_src.1, bf16[2,1024,1024]{2,1,0:T(8,128)(2,1)} %near_hbm.1, bf16[156,32,1024]{2,1,0:T(8,128)(2,1)} %left_hbm.1, ...), custom_call_target="tpu_custom_call" | custom-call | flops 800000000 | bytes 26000000 | tf_op jit(solution)/shard_map/hmatrix/pallas_call | solution.py:365
  123.2 2.3 %copy.11 = f32[16,16,1024]{2,1,0:T(8,128)} copy(f32[16,16,1024]{2,1,0:T(8,128)} %hmatrix.1) | data formatting | bytes 2097152

commit v2 on v0

v2 whole, which is shorter than its diff:
```python
import functools

import jax
import jax.numpy as jnp
from jax import lax
from jax.experimental import pallas as pl
from jax.experimental.pallas import tpu as pltpu
from jax.sharding import PartitionSpec as P

MESH = pl.DeviceIdType.MESH
BF = jnp.bfloat16
F32 = jnp.float32
I32 = jnp.int32
CL, RHS, LEAF, RANK = 16, 16, 1024, 32
NEAR, FAR, SLOTS = 2, 156, 8
ALL = NEAR + FAR
PAD = 160
PARTS = 8
THIN = LEAF // PARTS
WIDE = 2 * THIN
COLS = ((0, 384), (384, 384), (768, 256))
ORDER = ((0, 1, 2), (1, 2, 0), (2, 0, 1))
AXES = ((1, 2), (2, 1))


def kernel(
    xin, slots_in, near_row_in, near_src_in, far_row_in, far_src_in, near_hbm, left_hbm, right_hbm,
    out,
    x_v, near_row, near_src, far_row, far_src, slot_v, slot_o, slot_s,
    g0, g1, g2, t0, t1, t2, m0, m1, m2, i0, i1, i2,
    near, left, right, keys, tab_v, tab_s, inv_v, inv_r, inv_s,
    sums, proj, term, cum, send, r0, r1, r2, r3, r4, r5, r6, r7, fold, last, out_v,
    wsem, csem, ksem, s1s, s1r, sls, slr, s2s, s2r, s3s, s3r, ivs, ivr, o1s, o1r, o2s, o2r, osem,
):
    sfc, blk = lax.axis_index("sfc"), lax.axis_index("blk")
    core = sfc % 2
    pos = (sfc // 2, blk // 4, blk % 4)

    def moved(steps, flip=0):
        p = [(pos[a] + steps.get(a, 0)) % 4 for a in range(3)]
        return p[0] * 2 + (core + flip) % 2, p[1] * 4 + p[2]

    def remote(src, dst, ssem, rsem, to):
        return pltpu.make_async_remote_copy(
            src_ref=src, dst_ref=dst, send_sem=ssem, recv_sem=rsem, device_id=to, device_id_type=MESH
        )

    def starts(*copies):
        for c in copies:
            c.start()
        return list(copies)

    barrier = pltpu.get_barrier_semaphore()
    peers = [moved({}, 1)] + [moved({a: d}, f) for a in range(3) for d in range(1, 4) for f in range(2)]
    for to in peers:
        pl.semaphore_signal(barrier, inc=1, device_id=to, device_id_type=MESH)
    own_x, own_slot = starts(
        pltpu.make_async_copy(xin, x_v, csem.at[0]),
        pltpu.make_async_copy(slots_in, slot_o, csem.at[1]),
    )
    index = starts(
        pltpu.make_async_copy(near_row_in, near_row, csem.at[2]),
        pltpu.make_async_copy(near_src_in, near_src, csem.at[3]),
        pltpu.make_async_copy(far_row_in, far_row, csem.at[4]),
        pltpu.make_async_copy(far_src_in, far_src, csem.at[5]),
    )
    right[FAR:PAD] = jnp.zeros((PAD - FAR, RANK, LEAF), BF)
    left[FAR:PAD] = jnp.zeros((PAD - FAR, RANK, LEAF), BF)

    recv = (r0, r1, r2, r3, r4, r5, r6, r7)

    def clear(i, _):
        for buffer in recv:
            buffer[i // 4, i % 4, SLOTS] = jnp.zeros((RHS, THIN), BF)
        return 0

    lax.fori_loop(0, 16, clear, 0)
    own_x.wait()
    own_slot.wait()
    pl.semaphore_wait(barrier, len(peers))

    got = (g0, g1, g2)
    stage1, slots1 = [[], [], []], []
    for k in range(3):
        for d in (1, 3, 2):
            to = moved({ORDER[k][0]: d})
            slots1 += starts(remote(slots_in, slot_v.at[k, 3 - d], sls.at[k, d - 1], slr.at[k, d - 1], to))
    for d in (1, 3, 2):
        for k in (0, 1, 2):
            lo, wide = COLS[k]
            stage1[k] += starts(remote(
                x_v.at[:, :, pl.ds(lo, wide)], got[k].at[3 - d],
                s1s.at[k, d - 1], s1r.at[k, d - 1], moved({ORDER[k][0]: d}),
            ))

    pick, mid = (t0, t1, t2), (m0, m1, m2)
    stage2 = [[], [], []]

    def wanted(k, a, c, f, d):
        where = moved({ORDER[k][1]: d, ORDER[k][2]: c}, f)
        return where[0] * 16 + where[1]

    def choose(k, d, lo, n, value):
        def put(i, _):
            a, c, f = lo + i // 8, (i // 2) % 4, i % 2
            v = value(k, a, c, f, d)
            if d:
                pick[k][d - 1, a, c, f] = v
            elif k == 2:
                mid[k][0, a, c, f] = v
            else:
                mid[k][a, 0, c, f] = v
            return 0

        lax.fori_loop(0, 8 * n, put, 0, unroll=8)

    def pass_on(k, d, lo, n):
        group = 0 if lo == 0 else 1
        dst = mid[k].at[4 - d, pl.ds(lo, n)] if k == 2 else mid[k].at[pl.ds(lo, n), 4 - d]
        stage2[k] += starts(remote(
            pick[k].at[d - 1, pl.ds(lo, n)], dst,
            s2s.at[k, group, d - 1], s2r.at[k, group, d - 1], moved({ORDER[k][1]: d}),
        ))

    def value_own(k, a, c, f, d):
        lo, wide = COLS[k]
        return x_v[slot_o[0, wanted(k, 0, c, f, d)], :, lo : lo + wide]

    def value_got(k, a, c, f, d):
        return got[k][a - 1, slot_s[k, a - 1, 0, wanted(k, a, c, f, d)]]

    for d in (1, 3, 2):
        for k in (0, 1, 2):
            choose(k, d, 0, 1, value_own)
            pass_on(k, d, 0, 1)
    for k in range(3):
        choose(k, 0, 0, 1, value_own)
    weights = starts(
        pltpu.make_async_copy(right_hbm, right.at[pl.ds(0, FAR)], wsem.at[0]),
        pltpu.make_async_copy(left_hbm, left.at[pl.ds(0, FAR)], wsem.at[1]),
        pltpu.make_async_copy(near_hbm, near, wsem.at[2]),
    )
    for c in slots1:
        c.wait_recv()
    (slot_copy,) = starts(pltpu.make_async_copy(slot_v, slot_s, csem.at[6]))

    for c in index:
        c.wait()

    def fill_far(j, _):
        keys[pl.ds(j, 1), :] = jnp.full((1, 256), far_row[j], I32)
        return 0

    lax.fori_loop(0, FAR, fill_far, 0, unroll=4)
    for j in range(NEAR):
        keys[FAR + j : FAR + j + 1, :] = jnp.full((1, 256), near_row[j], I32)
    keys[ALL:PAD, :] = jnp.full((PAD - ALL, 256), 300, I32)
    row_c = keys[...]
    down = lax.broadcasted_iota(I32, (PAD, 256), 0)
    lane = lax.broadcasted_iota(I32, (PAD, 256), 1)
    row_r = jnp.sum(jnp.where(down == lane, row_c, 0), axis=0, keepdims=True)
    real = lane < PAD
    same = real & (row_r == row_c)
    less = real & (row_r < row_c)
    first_r = jnp.sum(jnp.where(same & (down < lane), 1, 0), axis=0, keepdims=True) == 0
    place = jnp.sum(jnp.where(less | (same & (lane < down)), 1, 0), axis=1, keepdims=True)
    final = jnp.sum(jnp.where(less | same, 1, 0), axis=1, keepdims=True) - 1
    slot = jnp.sum(jnp.where(less & first_r, 1, 0), axis=1, keepdims=True)
    here = place == lane
    tab_v[0:1, :] = jnp.sum(jnp.where(here, down, 0), axis=0, keepdims=True)
    tab_v[1:2, :] = jnp.sum(jnp.where(here, row_c, 0), axis=0, keepdims=True)
    tab_v[2:3, :] = jnp.max(jnp.where(slot == lane, final, 0), axis=0, keepdims=True)
    seat = jnp.max(jnp.where(row_c == lane, 8 - (slot & 7), 0), axis=0, keepdims=True)
    inv_v[0:1, :] = 8 - seat
    (tab_copy,) = starts(pltpu.make_async_copy(tab_v, tab_s, csem.at[7]))
    places = []
    for h in range(2):
        for d in range(1, 4):
            places += starts(remote(
                inv_v, inv_r.at[h, 4 - d], ivs.at[h, d - 1], ivr.at[h, d - 1], moved({AXES[h][0]: d})
            ))
        places += starts(pltpu.make_async_copy(inv_v, inv_r.at[h, 0], csem.at[8 + h]))

    inc = (i0, i1, i2)

    stage3, own3 = [[], [], []], [[], [], []]

    def deliver(k, group):
        part = 0 if group == 0 else pl.ds(1, 3)
        for d in (1, 3, 2, 0):
            e = (4 - d) % 4
            for f in range(2):
                if k == 2:
                    src, dst = mid[k].at[part, :, d, f], inc[k].at[part, f, e]
                elif k == 1:
                    src, dst = mid[k].at[:, part, d, f], inc[k].at[e, f, :, part]
                else:
                    src, dst = mid[k].at[:, part, d, f], inc[k].at[:, f, part, e]
                if d == 0 and f == 0:
                    own3[k].extend(starts(pltpu.make_async_copy(src, dst, ksem.at[k, group])))
                else:
                    n = d * 2 + f - 1
                    stage3[k].extend(starts(remote(
                        src, dst, s3s.at[k, group, n], s3r.at[k, group, n], moved({ORDER[k][2]: d}, f)
                    )))

    slot_copy.wait()
    for k in (2, 1, 0):
        for c in stage1[k]:
            c.wait_recv()
        for d in (1, 3, 2):
            choose(k, d, 1, 3, value_got)
            pass_on(k, d, 1, 3)
    for k in (2, 1, 0):
        choose(k, 0, 1, 3, value_got)
        deliver(k, 0)
    for k in (2, 1, 0):
        for c in stage2[k]:
            c.wait_recv()
        deliver(k, 1)

    def cluster(s, k):
        return inc[k][
            ((s >> 5) - pos[0]) & 3, ((s >> 4) - core) & 1, ((s >> 2) - pos[1]) & 3, (s - pos[2]) & 3
        ]

    diag = lax.broadcasted_iota(I32, (128, 256), 0) // 16 == lax.broadcasted_iota(I32, (128, 256), 1) // 32
    for c in weights:
        c.wait()
    for k in (2, 1, 0):
        for c in stage3[k]:
            c.wait_recv()
        for c in own3[k]:
            c.wait()

        def project(g, _, k=k):
            lo, wide = COLS[k]
            x = jnp.concatenate([cluster(far_src[jnp.minimum(8 * g + e, FAR - 1)], k) for e in range(8)], axis=0)
            w = right[pl.ds(8 * g, 8), :, lo : lo + wide].reshape(256, wide)
            r = lax.dot_general(x, w, (((1,), (1,)), ((), ())), preferred_element_type=F32)
            if k != 2:
                r += sums[g]
            if k != 0:
                sums[g] = r
            else:
                proj[g] = jnp.where(diag, r, 0.0).astype(BF)
            return 0

        lax.fori_loop(0, PAD // 8, project, 0, unroll=2)
    for c in places:
        c.wait()
    tab_copy.wait()
    (inv_copy,) = starts(pltpu.make_async_copy(inv_r, inv_s, csem.at[10]))

    out1 = []
    for q in range(PARTS // 2):
        cols = slice(WIDE * q, WIDE * (q + 1))

        def far(g, _, cols=cols):
            w = left[pl.ds(8 * g, 8), :, cols].reshape(256, WIDE)
            t = jnp.dot(proj[g], w, preferred_element_type=F32)
            term[pl.ds(8 * g, 8)] = t.reshape(8, RHS, WIDE)
            return 0

        lax.fori_loop(0, PAD // 8, far, 0, unroll=4)
        for n in range(NEAR):
            term[FAR + n] = lax.dot_general(
                jnp.concatenate([cluster(near_src[n], k) for k in range(3)], axis=1), near[n, cols, :], (((1,), (1,)), ((), ())), preferred_element_type=F32
            )

        def scan(i, carry):
            value, before = carry
            row = tab_s[1, i]
            value = value * (row == before).astype(F32) + term[tab_s[0, i]]
            cum[i] = value.astype(BF)
            return value, row

        lax.fori_loop(0, PAD, scan, (jnp.zeros((RHS, WIDE), F32), jnp.int32(-1)), unroll=8)

        for h in range(2):
            first, second = AXES[h]
            part = slice(THIN * h, THIN * (h + 1))
            out1.append([])
            for d in (1, 3, 2, 0):

                def load(i, _, q=2 * q + h, d=d, first=first, second=second, part=part):
                    w, t = i // 8, i % 8
                    value = cum[tab_s[2, moved({first: d, second: w})[1] * 8 + t], :, part]
                    if d == 0:
                        recv[q][0, w, t] = value
                    else:
                        send[q, d - 1, w, t] = value
                    return 0

                lax.fori_loop(0, 32, load, 0, unroll=8)
                if d:
                    out1[-1] += starts(remote(
                        send.at[2 * q + h, d - 1], recv[2 * q + h].at[4 - d, :, pl.ds(0, SLOTS)],
                        o1s.at[2 * q + h, d - 1], o1r.at[2 * q + h, d - 1], moved({first: d}),
                    ))

    inv_copy.wait()
    out2 = []
    for q in range(PARTS):
        h = q % 2
        first, second = AXES[h]
        for c in out1[q]:
            c.wait_recv()
        out2.append([])
        for d in (1, 3, 2, 0):

            def add(r, _, q=q, h=h, d=d, second=second):
                at = moved({second: d})[1] * 16 + r
                total = recv[q][0, d, inv_s[h, 0, 0, at]].astype(F32)
                for e in range(1, 4):
                    total += recv[q][e, d, inv_s[h, e, 0, at]].astype(F32)
                if d == 0:
                    out_v[q, r] = total
                else:
                    fold[q, d - 1, r] = total.astype(BF)
                return 0

            lax.fori_loop(0, CL, add, 0, unroll=4)
            if d:
                out2[q] += starts(remote(
                    fold.at[q, d - 1], last.at[q, d - 1], o2s.at[q, d - 1], o2r.at[q, d - 1], moved({second: d})
                ))
    results = []
    for q in range(PARTS):
        for c in out2[q]:
            c.wait_recv()

        def finish(r, _, q=q):
            total = out_v[q, r]
            for e in range(3):
                total += last[q, e, r].astype(F32)
            out_v[q, r] = total
            return 0

        lax.fori_loop(0, CL, finish, 0, unroll=4)
        results += starts(pltpu.make_async_copy(out_v.at[q], out.at[:, :, pl.ds(THIN * q, THIN)], osem.at[q]))

    for c in slots1 + sum(stage1, []) + sum(stage2, []) + sum(stage3, []) + sum(out1, []) + sum(out2, []):
        c.wait_send()
    for c in results:
        c.wait()


def local(xin, send_slot, near_blocks, near_row, near_src, far_left, far_right, far_row, far_src):
    hbm = pl.BlockSpec(memory_space=pl.ANY)
    widths = [w for _, w in COLS]
    dma, vmem, smem = pltpu.SemaphoreType.DMA, pltpu.VMEM, pltpu.SMEM
    scratch = [vmem((CL, RHS, LEAF), BF)]
    scratch += [smem((NEAR,), I32), smem((NEAR,), I32), smem((FAR,), I32), smem((FAR,), I32)]
    scratch += [vmem((3, 3, 1, 128), I32), smem((1, 128), I32), smem((3, 3, 1, 128), I32)]
    scratch += [vmem((3, CL, RHS, w), BF) for w in widths]
    scratch += [vmem((3, 4, 4, 2, RHS, w), BF) for w in widths]
    scratch += [vmem((4, 4, 4, 2, RHS, w), BF) for w in widths]
    scratch += [vmem((4, 2, 4, 4, RHS, w), BF) for w in widths]
    scratch += [
        vmem((NEAR, LEAF, LEAF), BF),
        vmem((PAD, RANK, LEAF), BF),
        vmem((PAD, RANK, LEAF), BF),
        vmem((PAD, 256), I32),
        vmem((8, 256), I32),
        smem((8, 256), I32),
        vmem((1, 256), I32),
        vmem((2, 4, 1, 256), I32),
        smem((2, 4, 1, 256), I32),
        vmem((PAD // 8, 128, 256), F32),
        vmem((PAD // 8, 128, 256), BF),
        vmem((PAD, RHS, WIDE), F32),
        vmem((PAD, RHS, WIDE), BF),
        vmem((PARTS, 3, 4, SLOTS, RHS, THIN), BF),
        *[vmem((4, 4, SLOTS + 1, RHS, THIN), BF)] * PARTS,
        vmem((PARTS, 3, CL, RHS, THIN), BF),
        vmem((PARTS, 3, CL, RHS, THIN), BF),
        vmem((PARTS, CL, RHS, THIN), F32),
    ]
    scratch += [dma((3,)), dma((11,)), dma((3, 2))] + [dma((3, 3))] * 4 + [dma((3, 2, 3))] * 2 + [dma((3, 2, 7))] * 2
    scratch += [dma((2, 3))] * 2 + [dma((PARTS, 3))] * 4 + [dma((PARTS,))]
    return pl.pallas_call(
        kernel,
        out_shape=jax.ShapeDtypeStruct((CL, RHS, LEAF), F32),
        in_specs=[hbm] * 9,
        out_specs=hbm,
        scratch_shapes=scratch,
        compiler_params=pltpu.CompilerParams(
            collective_id=0, has_side_effects=True, vmem_limit_bytes=60 << 20
        ),
        cost_estimate=pl.CostEstimate(flops=800_000_000, bytes_accessed=26_000_000, transcendentals=0),
        name="hmatrix",
    )(xin, send_slot, near_row, near_src, far_row, far_src, near_blocks, far_left, far_right)


def solution(mesh):
    both = ("sfc", "blk")
    placed = (
        P(both, None, None), P(both, None), P(both, None, None), P(both), P(both),
        P(both, None, None), P(both, None, None), P(both), P(both),
    )
    return jax.shard_map(local, mesh=mesh, in_specs=placed, out_specs=P(both, None, None), check_vma=False)
```

time: 273 us -> 102 us (0.37)
  waiting for transfers between devices: 160 us -> 0 us
  Pallas kernels: 0 us -> 100 us
  other arithmetic: 44 us -> 0 us
  local copies, waits for them, and re-layouts: 23.7 us -> 2.31 us
  matrix products: 19.7 us -> 0 us
  between operations: 13.5 us -> 0.01 us
  starting transfers between devices: 12 us -> 0 us
    reduce_scatter x1 -> x0, waiting for transfers between devices: 108 us -> none  [local(): lax.psum_scatter(partial_value, 'blk', scatter_dimension=0, tiled=True)]
    pallas_call x0 -> x1, Pallas kernels: none -> 100 us  [local(): pl.pallas_call(kernel, out_shape=jax.ShapeDtypeStruct((CL, RHS, LEAF), F3...]
    all_to_all x1 -> x0, waiting for transfers between devices: 51.8 us -> none  [local(): lax.all_to_all(outgoing, ('sfc', 'blk'), split_axis=0, concat_axis=0, til...]
    add x1 -> x0, other arithmetic: 33.2 us -> none  [local(): partial_value + jax.ops.segment_sum(far_term, far_row, num_segments=group...]
    dot_general x2 -> x0, matrix products: 19.7 us -> none  [the longest x1 16.3 us: local(): jnp.einsum('bki,brk->bri', far_left, projection, preferred_element_type=j...]
    gather x3 -> x0, local copies, waits for them, and re-layouts: 15.5 us -> none  [the longest x1 9.93 us: local(): far_inputs = incoming[far_src]]
    all_to_all x1 -> x0, starting transfers between devices: 12 us -> none  [local(): lax.all_to_all(outgoing, ('sfc', 'blk'), split_axis=0, concat_axis=0, til...]
    another operation x1 -> x0, other arithmetic: 10 us -> none
  transfers between devices with their start and end apart: 2 -> 0, of which waited for: 2 -> 0; matrix products, arithmetic and copies ran while one was open for 0% -> 0% of each run, Pallas kernels for 0% -> 0%
where the time goes in v2:
time: 102 us
  Pallas kernels  100 us (98%)
  local copies, waits for them, and re-layouts  2.31 us (2%)
    pallas_call x1, Pallas kernels, local(): pl.pallas_call(kernel, out_shape=jax.ShapeDtypeStruct((CL, RHS, LEAF), F3...  100 us
    unnamed x1, local copies, waits for them, and re-layouts  2.31 us

profile of v2, /device:TPU:1, one launch (start us, length us, event | category | flops | bytes accessed | tf_op | source)
XLA Modules:
  0.0 102.3 jit_solution(641673611257212131)
XLA Ops:
  0.0 100.0 %hmatrix.1 = f32[16,16,1024]{2,1,0:T(8,128)} custom-call(bf16[16,16,1024]{2,1,0:T(8,128)(2,1)} %xin.1, s32[1,128]{1,0:T(1,128)} %slots_in.1, s32[2]{0:T(128)} %near_row_in.1, s32[2]{0:T(128)} %near_src_in.1, s32[156]{0:T(256)} %far_row_in.1, s32[156]{0:T(256)} %far_src_in.1, bf16[2,1024,1024]{2,1,0:T(8,128)(2,1)} %near_hbm.1, ...), custom_call_target="tpu_custom_call" | custom-call | flops 800000000 | bytes 26000000 | tf_op jit(solution)/shard_map/hmatrix/pallas_call | solution.py:382
  100.0 2.3 %copy.11 = f32[16,16,1024]{2,1,0:T(8,128)} copy(f32[16,16,1024]{2,1,0:T(8,128)} %hmatrix.1) | data formatting | bytes 2097152

commit v3 on v2

--- a/solution.py
+++ b/solution.py
@@ -27,10 +27,10 @@
     xin, slots_in, near_row_in, near_src_in, far_row_in, far_src_in, near_hbm, left_hbm, right_hbm,
     out,
     x_v, near_row, near_src, far_row, far_src, slot_v, slot_o, slot_s,
-    g0, g1, g2, t0, t1, t2, m0, m1, m2, i0, i1, i2,
+    g01, g02, g03, g11, g12, g13, g21, g22, g23, t0, t1, t2, m0, m1, m2, i0, i1, i2,
     near, left, right, keys, tab_v, tab_s, inv_v, inv_r, inv_s,
-    sums, proj, term, cum, send, r0, r1, r2, r3, r4, r5, r6, r7, fold, last, out_v,
-    wsem, csem, ksem, s1s, s1r, sls, slr, s2s, s2r, s3s, s3r, ivs, ivr, o1s, o1r, o2s, o2r, osem,
+    proj, term, cum, send, r0, r1, r2, r3, r4, r5, r6, r7, fold, last, out_v,
+    wsem, csem, ksem, s1s, s1r, sls, slr, s2s, s2r, s3s, s3r, ivs, ivr, o1s, o1r, o2s, o2r,
 ):
     sfc, blk = lax.axis_index("sfc"), lax.axis_index("blk")
     core = sfc % 2
@@ -79,17 +79,17 @@
     own_slot.wait()
     pl.semaphore_wait(barrier, len(peers))
 
-    got = (g0, g1, g2)
-    stage1, slots1 = [[], [], []], []
+    got = ((None, g01, g02, g03), (None, g11, g12, g13), (None, g21, g22, g23))
+    stage1, passed, slots1 = [[], [], []], [[], [], []], []
     for k in range(3):
         for d in (1, 3, 2):
             to = moved({ORDER[k][0]: d})
             slots1 += starts(remote(slots_in, slot_v.at[k, 3 - d], sls.at[k, d - 1], slr.at[k, d - 1], to))
-    for d in (1, 3, 2):
-        for k in (0, 1, 2):
+    for d in (1, 3):
+        for k in (2, 1, 0):
             lo, wide = COLS[k]
             stage1[k] += starts(remote(
-                x_v.at[:, :, pl.ds(lo, wide)], got[k].at[3 - d],
+                x_v.at[:, :, pl.ds(lo, wide)], got[k][4 - d],
                 s1s.at[k, d - 1], s1r.at[k, d - 1], moved({ORDER[k][0]: d}),
             ))
 
@@ -100,10 +100,15 @@
         where = moved({ORDER[k][1]: d, ORDER[k][2]: c}, f)
         return where[0] * 16 + where[1]
 
-    def choose(k, d, lo, n, value):
+    def choose(k, d, a):
+        lo, wide = COLS[k]
+
         def put(i, _):
-            a, c, f = lo + i // 8, (i // 2) % 4, i % 2
-            v = value(k, a, c, f, d)
+            c, f = i // 2, i % 2
+            if a == 0:
+                v = x_v[slot_o[0, wanted(k, a, c, f, d)], :, lo : lo + wide]
+            else:
+                v = got[k][a][slot_s[k, a - 1, 0, wanted(k, a, c, f, d)]]
             if d:
                 pick[k][d - 1, a, c, f] = v
             elif k == 2:
@@ -112,38 +117,23 @@
                 mid[k][a, 0, c, f] = v
             return 0
 
-        lax.fori_loop(0, 8 * n, put, 0, unroll=8)
-
-    def pass_on(k, d, lo, n):
-        group = 0 if lo == 0 else 1
-        dst = mid[k].at[4 - d, pl.ds(lo, n)] if k == 2 else mid[k].at[pl.ds(lo, n), 4 - d]
+        lax.fori_loop(0, 8, put, 0, unroll=True)
+
+    def pass_on(k, d, a):
+        choose(k, d, a)
+        dst = mid[k].at[4 - d, a] if k == 2 else mid[k].at[a, 4 - d]
         stage2[k] += starts(remote(
-            pick[k].at[d - 1, pl.ds(lo, n)], dst,
-            s2s.at[k, group, d - 1], s2r.at[k, group, d - 1], moved({ORDER[k][1]: d}),
+            pick[k].at[d - 1, a], dst, s2s.at[k, a, d - 1], s2r.at[k, a, d - 1], moved({ORDER[k][1]: d})
         ))
 
-    def value_own(k, a, c, f, d):
-        lo, wide = COLS[k]
-        return x_v[slot_o[0, wanted(k, 0, c, f, d)], :, lo : lo + wide]
-
-    def value_got(k, a, c, f, d):
-        return got[k][a - 1, slot_s[k, a - 1, 0, wanted(k, a, c, f, d)]]
-
     for d in (1, 3, 2):
-        for k in (0, 1, 2):
-            choose(k, d, 0, 1, value_own)
-            pass_on(k, d, 0, 1)
-    for k in range(3):
-        choose(k, 0, 0, 1, value_own)
+        for k in (2, 1, 0):
+            pass_on(k, d, 0)
     weights = starts(
         pltpu.make_async_copy(right_hbm, right.at[pl.ds(0, FAR)], wsem.at[0]),
         pltpu.make_async_copy(left_hbm, left.at[pl.ds(0, FAR)], wsem.at[1]),
         pltpu.make_async_copy(near_hbm, near, wsem.at[2]),
     )
-    for c in slots1:
-        c.wait_recv()
-    (slot_copy,) = starts(pltpu.make_async_copy(slot_v, slot_s, csem.at[6]))
-
     for c in index:
         c.wait()
 
@@ -204,15 +194,30 @@
                         src, dst, s3s.at[k, group, n], s3r.at[k, group, n], moved({ORDER[k][2]: d}, f)
                     )))
 
-    slot_copy.wait()
     for k in (2, 1, 0):
         for c in stage1[k]:
             c.wait_recv()
-        for d in (1, 3, 2):
-            choose(k, d, 1, 3, value_got)
-            pass_on(k, d, 1, 3)
+        for n, (d, a) in enumerate(((1, 3), (3, 1))):
+            half = pl.ds(8 * n, 8)
+            passed[k] += starts(remote(
+                got[k][a].at[half], got[k][2].at[half],
+                s1s.at[k, n + 3], s1r.at[k, n + 3], moved({ORDER[k][0]: d}),
+            ))
+    for c in slots1:
+        c.wait_recv()
+    (slot_copy,) = starts(pltpu.make_async_copy(slot_v, slot_s, csem.at[6]))
+
+    slot_copy.wait()
+    for a in (1, 3, 2):
+        for k in (2, 1, 0):
+            if a == 2:
+                for c in passed[k]:
+                    c.wait_recv()
+            for d in (1, 3, 2):
+                pass_on(k, d, a)
     for k in (2, 1, 0):
-        choose(k, 0, 1, 3, value_got)
+        for a in range(4):
+            choose(k, 0, a)
         deliver(k, 0)
     for k in (2, 1, 0):
         for c in stage2[k]:
@@ -239,14 +244,14 @@
             w = right[pl.ds(8 * g, 8), :, lo : lo + wide].reshape(256, wide)
             r = lax.dot_general(x, w, (((1,), (1,)), ((), ())), preferred_element_type=F32)
             if k != 2:
-                r += sums[g]
+                r += term[pl.ds(8 * g, 8)].reshape(128, 256)
             if k != 0:
-                sums[g] = r
+                term[pl.ds(8 * g, 8)] = r.reshape(8, RHS, 256)
             else:
                 proj[g] = jnp.where(diag, r, 0.0).astype(BF)
             return 0
 
-        lax.fori_loop(0, PAD // 8, project, 0, unroll=2)
+        lax.fori_loop(0, PAD // 8, project, 0, unroll=20)
     for c in places:
         c.wait()
     tab_copy.wait()
@@ -262,7 +267,7 @@
             term[pl.ds(8 * g, 8)] = t.reshape(8, RHS, WIDE)
             return 0
 
-        lax.fori_loop(0, PAD // 8, far, 0, unroll=4)
+        lax.fori_loop(0, PAD // 8, far, 0, unroll=20)
         for n in range(NEAR):
             term[FAR + n] = lax.dot_general(
                 jnp.concatenate([cluster(near_src[n], k) for k in range(3)], axis=1), near[n, cols, :], (((1,), (1,)), ((), ())), preferred_element_type=F32
@@ -275,7 +280,7 @@
             cum[i] = value.astype(BF)
             return value, row
 
-        lax.fori_loop(0, PAD, scan, (jnp.zeros((RHS, WIDE), F32), jnp.int32(-1)), unroll=8)
+        lax.fori_loop(0, PAD, scan, (jnp.zeros((RHS, WIDE), F32), jnp.int32(-1)), unroll=16)
 
         for h in range(2):
             first, second = AXES[h]
@@ -325,7 +330,6 @@
                 out2[q] += starts(remote(
                     fold.at[q, d - 1], last.at[q, d - 1], o2s.at[q, d - 1], o2r.at[q, d - 1], moved({second: d})
                 ))
-    results = []
     for q in range(PARTS):
         for c in out2[q]:
             c.wait_recv()
@@ -334,16 +338,13 @@
             total = out_v[q, r]
             for e in range(3):
                 total += last[q, e, r].astype(F32)
-            out_v[q, r] = total
+            out[r, :, THIN * q : THIN * (q + 1)] = total
             return 0
 
         lax.fori_loop(0, CL, finish, 0, unroll=4)
-        results += starts(pltpu.make_async_copy(out_v.at[q], out.at[:, :, pl.ds(THIN * q, THIN)], osem.at[q]))
-
-    for c in slots1 + sum(stage1, []) + sum(stage2, []) + sum(stage3, []) + sum(out1, []) + sum(out2, []):
+
+    for c in slots1 + sum(stage1, []) + sum(passed, []) + sum(stage2, []) + sum(stage3, []) + sum(out1, []) + sum(out2, []):
         c.wait_send()
-    for c in results:
-        c.wait()
 
 
 def local(xin, send_slot, near_blocks, near_row, near_src, far_left, far_right, far_row, far_src):
@@ -353,7 +354,7 @@
     scratch = [vmem((CL, RHS, LEAF), BF)]
     scratch += [smem((NEAR,), I32), smem((NEAR,), I32), smem((FAR,), I32), smem((FAR,), I32)]
     scratch += [vmem((3, 3, 1, 128), I32), smem((1, 128), I32), smem((3, 3, 1, 128), I32)]
-    scratch += [vmem((3, CL, RHS, w), BF) for w in widths]
+    scratch += [vmem((CL, RHS, w), BF) for w in widths for _ in range(3)]
     scratch += [vmem((3, 4, 4, 2, RHS, w), BF) for w in widths]
     scratch += [vmem((4, 4, 4, 2, RHS, w), BF) for w in widths]
     scratch += [vmem((4, 2, 4, 4, RHS, w), BF) for w in widths]
@@ -367,7 +368,6 @@
         vmem((1, 256), I32),
         vmem((2, 4, 1, 256), I32),
         smem((2, 4, 1, 256), I32),
-        vmem((PAD // 8, 128, 256), F32),
         vmem((PAD // 8, 128, 256), BF),
         vmem((PAD, RHS, WIDE), F32),
         vmem((PAD, RHS, WIDE), BF),
@@ -377,16 +377,16 @@
         vmem((PARTS, 3, CL, RHS, THIN), BF),
         vmem((PARTS, CL, RHS, THIN), F32),
     ]
-    scratch += [dma((3,)), dma((11,)), dma((3, 2))] + [dma((3, 3))] * 4 + [dma((3, 2, 3))] * 2 + [dma((3, 2, 7))] * 2
-    scratch += [dma((2, 3))] * 2 + [dma((PARTS, 3))] * 4 + [dma((PARTS,))]
+    scratch += [dma((3,)), dma((11,)), dma((3, 2))] + [dma((3, 5))] * 2 + [dma((3, 3))] * 2 + [dma((3, 4, 3))] * 2 + [dma((3, 2, 7))] * 2
+    scratch += [dma((2, 3))] * 2 + [dma((PARTS, 3))] * 4
     return pl.pallas_call(
         kernel,
-        out_shape=jax.ShapeDtypeStruct((CL, RHS, LEAF), F32),
+        out_shape=pltpu.VMEM((CL, RHS, LEAF), F32),
         in_specs=[hbm] * 9,
-        out_specs=hbm,
+        out_specs=pl.BlockSpec(memory_space=pltpu.VMEM),
         scratch_shapes=scratch,
         compiler_params=pltpu.CompilerParams(
-            collective_id=0, has_side_effects=True, vmem_limit_bytes=60 << 20
+            collective_id=0, has_side_effects=True, vmem_limit_bytes=56 << 20
         ),
         cost_estimate=pl.CostEstimate(flops=800_000_000, bytes_accessed=26_000_000, transcendentals=0),
         name="hmatrix",

time: 102 us -> 93.7 us (0.919)
  Pallas kernels: 100 us -> 92.6 us
  local copies, waits for them, and re-layouts: 2.31 us -> 0.97 us
    pallas_call x1, Pallas kernels: 100 us -> 92.6 us  [local(): pl.pallas_call(kernel, out_shape=pltpu.VMEM((CL, RHS, LEAF), F32), in_spe...]
    unnamed x1, local copies, waits for them, and re-layouts: 2.31 us -> 0.97 us
where the time goes in v3:
time: 93.7 us; the launch traced here: 93.6 us
  Pallas kernels  92.6 us (99%)
  local copies, waits for them, and re-layouts  0.97 us (1%)
    pallas_call x1, Pallas kernels, local(): pl.pallas_call(kernel, out_shape=pltpu.VMEM((CL, RHS, LEAF), F32), in_spe...  92.6 us

profile of v3, /device:TPU:1, one launch (start us, length us, event | category | flops | bytes accessed | tf_op | source)
XLA Modules:
  0.0 93.6 jit_solution(8118608922378567333)
XLA Ops:
  0.0 92.6 %hmatrix.1 = f32[16,16,1024]{2,1,0:T(8,128)S(1)} custom-call(bf16[16,16,1024]{2,1,0:T(8,128)(2,1)} %xin.1, s32[1,128]{1,0:T(1,128)} %slots_in.1, s32[2]{0:T(128)} %near_row_in.1, s32[2]{0:T(128)} %near_src_in.1, s32[156]{0:T(256)} %far_row_in.1, s32[156]{0:T(256)} %far_src_in.1, bf16[2,1024,1024]{2,1,0:T(8,128)(2,1)} %near_hbm.1, ...), custom_call_target="tpu_custom_call" | custom-call | flops 800000000 | bytes 26000000 | tf_op jit(solution)/shard_map/hmatrix/pallas_call | solution.py:382
  92.6 1.0 %copy.11 = f32[16,16,1024]{2,1,0:T(8,128)} copy(f32[16,16,1024]{2,1,0:T(8,128)S(1)} %hmatrix.1) | data formatting | bytes 2097152

commit v4 on v3

--- a/solution.py
+++ b/solution.py
@@ -141,7 +141,7 @@
         keys[pl.ds(j, 1), :] = jnp.full((1, 256), far_row[j], I32)
         return 0
 
-    lax.fori_loop(0, FAR, fill_far, 0, unroll=4)
+    lax.fori_loop(0, FAR, fill_far, 0, unroll=12)
     for j in range(NEAR):
         keys[FAR + j : FAR + j + 1, :] = jnp.full((1, 256), near_row[j], I32)
     keys[ALL:PAD, :] = jnp.full((PAD - ALL, 256), 300, I32)
@@ -280,7 +280,7 @@
             cum[i] = value.astype(BF)
             return value, row
 
-        lax.fori_loop(0, PAD, scan, (jnp.zeros((RHS, WIDE), F32), jnp.int32(-1)), unroll=16)
+        lax.fori_loop(0, PAD, scan, (jnp.zeros((RHS, WIDE), F32), jnp.int32(-1)), unroll=32)
 
         for h in range(2):
             first, second = AXES[h]
@@ -297,7 +297,7 @@
                         send[q, d - 1, w, t] = value
                     return 0
 
-                lax.fori_loop(0, 32, load, 0, unroll=8)
+                lax.fori_loop(0, 32, load, 0, unroll=16)
                 if d:
                     out1[-1] += starts(remote(
                         send.at[2 * q + h, d - 1], recv[2 * q + h].at[4 - d, :, pl.ds(0, SLOTS)],
@@ -325,7 +325,7 @@
                     fold[q, d - 1, r] = total.astype(BF)
                 return 0
 
-            lax.fori_loop(0, CL, add, 0, unroll=4)
+            lax.fori_loop(0, CL, add, 0, unroll=16)
             if d:
                 out2[q] += starts(remote(
                     fold.at[q, d - 1], last.at[q, d - 1], o2s.at[q, d - 1], o2r.at[q, d - 1], moved({second: d})
@@ -341,7 +341,7 @@
             out[r, :, THIN * q : THIN * (q + 1)] = total
             return 0
 
-        lax.fori_loop(0, CL, finish, 0, unroll=4)
+        lax.fori_loop(0, CL, finish, 0, unroll=16)
 
     for c in slots1 + sum(stage1, []) + sum(passed, []) + sum(stage2, []) + sum(stage3, []) + sum(out1, []) + sum(out2, []):
         c.wait_send()

time: 93.7 us -> 93.6 us (level)
  no operation moved by 1% of the time
where the time goes in v4:
time: 93.6 us; the launch traced here: 93.4 us
  Pallas kernels  92.5 us (99%)
  local copies, waits for them, and re-layouts  0.97 us (1%)
    pallas_call x1, Pallas kernels, local(): pl.pallas_call(kernel, out_shape=pltpu.VMEM((CL, RHS, LEAF), F32), in_spe...  92.5 us

profile of v4, /device:TPU:1, one launch (start us, length us, event | category | flops | bytes accessed | tf_op | source)
XLA Modules:
  0.0 93.4 jit_solution(6434689743358253417)
XLA Ops:
  0.0 92.5 %hmatrix.1 = f32[16,16,1024]{2,1,0:T(8,128)S(1)} custom-call(bf16[16,16,1024]{2,1,0:T(8,128)(2,1)} %xin.1, s32[1,128]{1,0:T(1,128)} %slots_in.1, s32[2]{0:T(128)} %near_row_in.1, s32[2]{0:T(128)} %near_src_in.1, s32[156]{0:T(256)} %far_row_in.1, s32[156]{0:T(256)} %far_src_in.1, bf16[2,1024,1024]{2,1,0:T(8,128)(2,1)} %near_hbm.1, ...), custom_call_target="tpu_custom_call" | custom-call | flops 800000000 | bytes 26000000 | tf_op jit(solution)/shard_map/hmatrix/pallas_call | solution.py:382
  92.5 1.0 %copy.11 = f32[16,16,1024]{2,1,0:T(8,128)} copy(f32[16,16,1024]{2,1,0:T(8,128)S(1)} %hmatrix.1) | data formatting | bytes 2097152
